TPU v7x, 32 devices: a whole 2x2x4 slice. The times are simulated.
32 devices in a mesh: groups: 2 (over x), col: 16 (over z, y, core).
Axes of the slice: x: 2, y: 2, z: 4, core: 2. Of those that a mesh axis runs over, the one named last changes fastest.
Arguments:
- slab: float32 [2, 2048, 4096], P(None, 'groups', 'col'), parts along dimension 1, may hold values from -6 to 6
- block_on: int32 [16, 32], P('groups', 'col'), parts along dimension 0, may hold values 0 or 1
- block_band: int32 [16, 32], P('groups', 'col'), parts along dimension 0, may hold values from 0 to 3
- band_gain: float32 [4], replicated, may hold values from 0.25 to 2
Outputs:
- spectra: float32 [2, 2048, 4096], P(None, 'groups', 'col'), parts along dimension 1
There are 2 independent parts, one for each index of `groups`. A program takes and returns all parts, laid end to end along the dimension named above; an argument that names none is the same for every part. Nothing has to cross between parts.
All inputs are finite; a program needn't handle non-finite values. No bound on the sum of `block_on` on one device may be relied on, other than what follows from the above.
Results may differ from a plain program's by a relative error of at most 0.00007.
Values sent between devices are 32-bit elements; how exact they have to be, the bound alone decides.
A program may use at most 64 MiB of HBM per device.

v0:
```python
import math

import jax
import jax.numpy as jnp
from jax import lax
from jax.sharding import PartitionSpec as P

BLOCK = 128


def phase_table(first_index, second_index, length):
    product = first_index[:, None] * second_index[None, :] % length
    angles = product.astype(jnp.float32) * (2.0 * math.pi / length)
    return (jnp.cos(angles), -jnp.sin(angles))


def contract(stacked, table, formula):
    cosine_table, sine_table = table
    real_part = jnp.einsum(
        formula, stacked[0], cosine_table, precision=lax.Precision.HIGHEST
    ) - jnp.einsum(formula, stacked[1], sine_table, precision=lax.Precision.HIGHEST)
    imag_part = jnp.einsum(
        formula, stacked[0], sine_table, precision=lax.Precision.HIGHEST
    ) + jnp.einsum(formula, stacked[1], cosine_table, precision=lax.Precision.HIGHEST)
    return jnp.stack([real_part, imag_part])


def rotate(stacked, table):
    cosine_table, sine_table = table
    real_part = stacked[0] * cosine_table - stacked[1] * sine_table
    imag_part = stacked[0] * sine_table + stacked[1] * cosine_table
    return jnp.stack([real_part, imag_part])


def shards(slab, block_on, block_band, band_gain):
    devices = lax.axis_size("col")
    rows_total = slab.shape[1]
    shard_cols = slab.shape[2]
    length = shard_cols * devices
    rows_here = rows_total // devices
    factor = 1.0 / math.sqrt(length)
    first_len = BLOCK
    second_len = length // first_len
    first_iota = jnp.arange(first_len, dtype=jnp.int32)
    second_iota = jnp.arange(second_len, dtype=jnp.int32)
    table_one = phase_table(first_iota, first_iota, first_len)
    table_middle = phase_table(first_iota, second_iota, length)
    table_two = phase_table(second_iota, second_iota, second_len)
    received = lax.all_to_all(
        slab.reshape(2, devices, rows_here, shard_cols),
        "col",
        split_axis=1,
        concat_axis=3,
        tiled=True,
    )
    row_count = received.shape[2]
    square = received[:, 0].reshape(2, row_count, first_len, second_len)
    mixture = contract(square, table_one, "rab,ak->rkb")
    mixture = rotate(mixture, table_middle)
    result = contract(mixture, table_two, "rkb,bm->rmk")
    whole = result.reshape(2, 1, row_count, length)
    whole = whole.reshape(2, rows_here, devices, shard_cols)
    spectrum = lax.all_to_all(whole, "col", split_axis=2, concat_axis=1, tiled=True).reshape(
        2, rows_total, shard_cols
    )
    choose = (block_band[..., None] == jnp.arange(band_gain.shape[0], dtype=jnp.int32)).astype(
        jnp.float32
    )
    weight = block_on.astype(jnp.float32) * jnp.sum(choose * band_gain, axis=-1) * factor
    row_blocks = rows_total // BLOCK
    col_blocks = shard_cols // BLOCK
    masked = (
        spectrum.reshape(2, row_blocks, BLOCK, col_blocks, BLOCK) * weight[None, :, None, :, None]
    )
    return masked.reshape(2, rows_total, shard_cols)


def solution(mesh):
    placed = (P(None, "groups", "col"), P("groups", "col"), P("groups", "col"), P())
    return jax.shard_map(
        shards, mesh=mesh, in_specs=placed, out_specs=P(None, "groups", "col"), check_vma=False
    )
```

profile of v0, /device:TPU:13, one launch (start us, length us, event | category | flops | bytes accessed | tf_op | source)
XLA Modules:
  0.0 138.5 jit_solution(2403043482625478237)
XLA Ops:
  0.0 3.1 %copy.54 = f32[2,16,64,256]{3,2,0,1:T(8,128)} copy(f32[2,16,64,256]{3,2,1,0:T(8,128)} %bitcast.56) | data formatting | bytes 4194304 | tf_op jit(solution)/shard_map/reshape | solution.py:50
  3.1 6.6 %all-to-all-start = ((f32[2,16,64,256]{3,2,0,1:T(8,128)}), f32[2,16,64,256]{3,2,0,1:T(8,128)S(1)}, u32[]{:S(2)}, u32[]{:S(2)}) async-start(f32[2,16,64,256]{3,2,0,1:T(8,128)} %copy.54), calls=%async_computation | async-start | bytes 4194304 | tf_op jit(solution)/shard_map/all_to_all | solution.py:49
  9.7 0.1 sine_negate_fusion.4
  9.8 47.3 %all-to-all-done = f32[2,16,64,256]{3,2,0,1:T(8,128)S(1)} async-done(((f32[2,16,64,256]{3,2,0,1:T(8,128)}), f32[2,16,64,256]{3,2,0,1:T(8,128)S(1)}, u32[]{:S(2)}, u32[]{:S(2)}) %all-to-all-start) | async-done | bytes 2097184 | tf_op jit(solution)/shard_map/all_to_all | solution.py:49
  57.1 1.2 fusion.79
  58.3 0.6 copy.55
  58.9 1.3 copy.56
  60.2 1.2 fusion.11
  61.4 2.2 %fusion.15 = f32[128,64,32]{0,1,2:T(8,128)} fusion(f32[64,128,32]{1,0,2:T(8,128)S(1)} %copy.56), kind=kOutput, calls=%fused_computation.27 | convolution fusion | flops 402882560 | bytes 2097152 | tf_op jit(solution)/shard_map/rab,ak->rkb/dot_general | solution.py:19
  63.6 1.9 %copy.57 = f32[1,1,64,16,256]{2,4,3,1,0:T(8,128)} copy(f32[1,1,64,16,256]{4,2,0,3,1:T(8,128)S(1)} %copy-done.1) | data formatting | bytes 2097152 | tf_op jit(solution)/shard_map/slice | solution.py:21
  65.6 2.7 %copy.58 = f32[64,128,32]{1,0,2:T(8,128)S(1)} copy(f32[64,128,32]{0,2,1:T(8,128)} %bitcast.52) | data formatting | bytes 2097152 | tf_op jit(solution)/shard_map/squeeze | solution.py:21
  68.2 1.3 convolution_add_fusion.1
  69.5 1.4 %add_bitcast_fusion = (f32[64,128,32]{1,0,2:T(8,128)S(1)}, f32[64,128,32]{1,0,2:T(8,128)S(1)}) fusion(f32[128,64,32]{0,1,2:T(8,128)S(1)} %convolution_add_fusion.1, f32[128,32]{0,1:T(8,128)S(1)} %get-tuple-element.9, f32[128,32]{0,1:T(8,128)S(1)} %get-tuple-element.10, f32[128,64,32]{0,1,2:T(8,128)S(1)} %copy-done, f32[64,128,32]{1,0,2:T(8,128)S(1)} %copy.58), kind=kOutput, calls=%fused_computation.9 | convolution fusion | flops 404733952 | bytes 5275648 | tf_op jit(solution)/shard_map/rab,ak->rkb/dot_general | solution.py:21
  70.9 1.6 %fusion.6 = f32[32,64,128]{2,0,1:T(8,128)S(1)} fusion(f32[64,128,32]{1,0,2:T(8,128)S(1)} %get-tuple-element.6), kind=kOutput, calls=%fused_computation.15 | convolution fusion | flops 100677632 | bytes 2097152 | tf_op jit(solution)/shard_map/rkb,bm->rmk/dot_general | solution.py:19
  72.5 1.6 %fusion.4 = f32[32,64,128]{2,0,1:T(8,128)S(1)} fusion(f32[64,128,32]{1,0,2:T(8,128)S(1)} %get-tuple-element.6), kind=kOutput, calls=%fused_computation.13 | convolution fusion | flops 100678656 | bytes 2097152 | tf_op jit(solution)/shard_map/rkb,bm->rmk/dot_general | solution.py:22
  74.1 1.8 %fusion.1 = f32[64,32,128]{2,1,0:T(8,128)S(1)} fusion(f32[32,64,128]{2,0,1:T(8,128)S(1)} %fusion.6, f32[64,128,32]{1,0,2:T(8,128)S(1)} %get-tuple-element.5), kind=kOutput, calls=%fused_computation.5 | convolution fusion | flops 100940800 | bytes 3145728 | tf_op jit(solution)/shard_map/rkb,bm->rmk/dot_general | solution.py:21
  75.9 1.3 stack.9
  77.2 2.8 %copy.65 = f32[1,64,16,256]{3,1,0,2:T(8,128)} copy(f32[1,64,16,256]{3,2,1,0:T(8,128)} %stack.9) | data formatting | bytes 2097152 | tf_op jit(solution)/shard_map/stack | solution.py:25
  80.0 1.6 %fusion = f32[64,32,128]{2,1,0:T(8,128)S(1)} fusion(f32[32,64,128]{2,0,1:T(8,128)S(1)} %fusion.4, f32[64,128,32]{1,0,2:T(8,128)S(1)} %get-tuple-element.5), kind=kOutput, calls=%fused_computation.3 | convolution fusion | flops 100939776 | bytes 3145728 | tf_op jit(solution)/shard_map/rkb,bm->rmk/dot_general | solution.py:24
  81.6 0.3 stack.10
  81.9 0.6 copy.66
  82.5 0.3 copy-done.2
  82.8 1.5 %pad_maximum_fusion = f32[2,64,16,256]{3,1,0,2:T(8,128)} fusion(f32[1,64,16,256]{3,1,0,2:T(8,128)S(1)} %copy.66, f32[1,64,16,256]{3,1,0,2:T(8,128)S(1)} %copy-done.2), kind=kLoop, calls=%fused_computation | loop fusion | flops 524288 | bytes 4194304 | tf_op jit(solution)/shard_map/stack | solution.py:25
  84.3 5.1 %all-to-all-start.1 = ((f32[2,64,16,256]{3,1,0,2:T(8,128)}), f32[2,64,16,256]{3,1,0,2:T(8,128)S(1)}, u32[]{:S(2)}, u32[]{:S(2)}) async-start(f32[2,64,16,256]{3,1,0,2:T(8,128)} %pad_maximum_fusion), calls=%async_computation.1 | async-start | bytes 4194304 | tf_op jit(solution)/shard_map/all_to_all | solution.py:63
  89.4 0.1 select_reduce_fusion
  89.5 0.0 copy-done.3
  89.5 0.1 copy.68
  89.5 0.3 mul.231
  89.9 0.1 copy.79
  90.0 46.8 %all-to-all-done.1 = f32[2,64,16,256]{3,1,0,2:T(8,128)S(1)} async-done(((f32[2,64,16,256]{3,1,0,2:T(8,128)}), f32[2,64,16,256]{3,1,0,2:T(8,128)S(1)}, u32[]{:S(2)}, u32[]{:S(2)}) %all-to-all-start.1) | async-done | bytes 2097184 | tf_op jit(solution)/shard_map/all_to_all | solution.py:63
  136.8 0.2 copy.67
  137.0 1.5 %bitcast_multiply_fusion = f32[2,1024,256]{2,1,0:T(8,128)} fusion(f32[2,64,16,256]{3,1,2,0:T(8,128)S(1)} %copy.67, f32[1024,256]{1,0:T(8,128)S(1)} %bitcast.54), kind=kLoop, calls=%fused_computation.1 | loop fusion | flops 524288 | bytes 5242880 | tf_op jit(solution)/shard_map/mul | solution.py:73
  (11 shorter events, 0.0 us)
Async XLA Ops:
  3.1 54.0 %all-to-all-start = ((f32[2,16,64,256]{3,2,0,1:T(8,128)}), f32[2,16,64,256]{3,2,0,1:T(8,128)S(1)}, u32[]{:S(2)}, u32[]{:S(2)}) async-start(f32[2,16,64,256]{3,2,0,1:T(8,128)} %copy.54), calls=%async_computation | async-start | bytes 4194304 | tf_op jit(solution)/shard_map/all_to_all | solution.py:49
  60.2 3.5 %copy-start.1 = (f32[1,1,64,16,256]{4,2,0,3,1:T(8,128)S(1)}, f32[1,1,64,16,256]{4,2,0,3,1:T(8,128)}, u32[]{:S(2)}) copy-start(f32[1,1,64,16,256]{4,2,0,3,1:T(8,128)} %get-tuple-element.7) | copy-start | bytes 3145732
  68.2 1.3 copy-start
  81.6 1.2 copy-start.2
  84.3 5.1 %copy-start.4 = (s32[8,2]{0,1:T(2,128)S(1)}, s32[8,2]{0,1:T(2,128)}, u32[]{:S(2)}) copy-start(s32[8,2]{0,1:T(2,128)} %param.6) | copy-start | bytes 196
  84.3 5.1 %copy-start.5 = (f32[4]{0:T(128)S(1)}, f32[4]{0:T(128)}, u32[]{:S(2)}) copy-start(f32[4]{0:T(128)} %param.7) | copy-start | bytes 52
  84.3 5.2 %copy-start.3 = (s32[8,2]{0,1:T(2,128)S(1)}, s32[8,2]{0,1:T(2,128)}, u32[]{:S(2)}) copy-start(s32[8,2]{0,1:T(2,128)} %param.5) | copy-start | bytes 196
  84.3 52.5 %all-to-all-start.1 = ((f32[2,64,16,256]{3,1,0,2:T(8,128)}), f32[2,64,16,256]{3,1,0,2:T(8,128)S(1)}, u32[]{:S(2)}, u32[]{:S(2)}) async-start(f32[2,64,16,256]{3,1,0,2:T(8,128)} %pad_maximum_fusion), calls=%async_computation.1 | async-start | bytes 4194304 | tf_op jit(solution)/shard_map/all_to_all | solution.py:63
where the time goes:
time: 139 us
  waiting for transfers between devices  94.1 us (68%)
  local copies, waits for them, and re-layouts  16.8 us (12%)
  matrix products  12.7 us (9%)
  starting transfers between devices  11.6 us (8%)
  other arithmetic  3.18 us (2%)
    all_to_all x1, waiting for transfers between devices, shards(): lax.all_to_all(slab.reshape(2, devices, rows_here, shard_cols), 'col', sp...  47.3 us
    all_to_all x1, waiting for transfers between devices, shards(): lax.all_to_all(whole, 'col', split_axis=2, concat_axis=1, tiled=True)  46.8 us
    all_to_all x1, starting transfers between devices, shards(): lax.all_to_all(slab.reshape(2, devices, rows_here, shard_cols), 'col', sp...  6.55 us
    all_to_all x1, starting transfers between devices, shards(): lax.all_to_all(whole, 'col', split_axis=2, concat_axis=1, tiled=True)  5.06 us
    another operation x4, local copies, waits for them, and re-layouts, contract(): return jnp.stack([real_part, imag_part])  4.98 us
    dot_general x2, matrix products, contract(): jnp.einsum(formula, stacked[0], cosine_table, precision=lax.Precision.HIG...  3.8 us
    dot_general x2, matrix products, contract(): jnp.einsum(formula, stacked[1], sine_table, precision=lax.Precision.HIGHEST)  3.18 us
    reshape x1, local copies, waits for them, and re-layouts, shards(): slab.reshape(2, devices, rows_here, shard_cols)  3.13 us
  transfers between devices with their start and end apart: 2, of which 2 were waited for; matrix products, arithmetic and copies ran while one was open for 0% of the time, Pallas kernels for 0%

commit v1 on v0

v1 whole, which is shorter than its diff:
```python
import functools
import math

import jax
import jax.numpy as jnp
import ml_dtypes
import numpy as np
from jax import lax
from jax.experimental import pallas as pl
from jax.experimental.pallas import tpu as pltpu
from jax.sharding import PartitionSpec as P

BLOCK = 128
LANES = 128
MESH = pl.DeviceIdType.MESH


def butterflies(planes):
    count = len(planes)
    if count == 1:
        return planes
    even = butterflies(planes[0::2])
    odd = butterflies(planes[1::2])
    low, high = [], []
    for k in range(count // 2):
        er, ei = even[k]
        xr, xi = odd[k]
        if k == 0:
            tr, ti = xr, xi
        elif 4 * k == count:
            tr, ti = xi, -xr
        else:
            c = math.cos(2.0 * math.pi * k / count)
            s = -math.sin(2.0 * math.pi * k / count)
            if 8 * k == count:
                tr, ti = c * (xr + xi), c * (xi - xr)
            elif 8 * k == 3 * count:
                tr, ti = s * (xr - xi), s * (xr + xi)
            else:
                tr, ti = c * xr - s * xi, c * xi + s * xr
        low.append((er + tr, ei + ti))
        high.append((er - tr, ei - ti))
    return low + high


def kernel(
    n, chunks, rows, x_ref, tw_ref, whi_ref, wlo_ref, out_ref,
    recv, mid, spread, done, s1, r1, s2, r2, own1, own2,
):
    me = lax.axis_index("col")
    rows_here = chunks * rows
    width = x_ref.shape[2]

    barrier = pltpu.get_barrier_semaphore()

    def greet(t, carry):
        pl.semaphore_signal(
            barrier, inc=1, device_id={"col": lax.rem(me + t, n)}, device_id_type=MESH
        )
        return carry

    lax.fori_loop(1, n, greet, 0)

    def part_of(ref, owner, c):
        start = pl.multiple_of(owner * rows_here + c * rows, rows)
        return ref.at[:, pl.ds(start, rows), :]

    def first(c, t):
        peer = lax.rem(me + t, n)
        return pltpu.make_async_remote_copy(
            src_ref=part_of(x_ref, peer, c),
            dst_ref=recv.at[c, me],
            send_sem=s1.at[c, t],
            recv_sem=r1.at[c, t],
            device_id={"col": peer},
            device_id_type=MESH,
        )

    def second(c, t):
        peer = lax.rem(me + t, n)
        return pltpu.make_async_remote_copy(
            src_ref=done.at[c, peer],
            dst_ref=part_of(out_ref, me, c),
            send_sem=s2.at[c, t],
            recv_sem=r2.at[c, t],
            device_id={"col": peer},
            device_id_type=MESH,
        )

    def own_in(c):
        return pltpu.make_async_copy(part_of(x_ref, me, c), recv.at[c, me], own1.at[c])

    def own_out(c):
        return pltpu.make_async_copy(done.at[c, me], part_of(out_ref, me, c), own2.at[c])

    for c in range(chunks):
        own_in(c).start()
    pl.semaphore_wait(barrier, n - 1)
    for c in range(chunks):

        def send_first(t, carry, c=c):
            first(c, t).start()
            return carry

        lax.fori_loop(1, n, send_first, 0)

    for c in range(chunks):
        own_in(c).wait()

        def take_first(t, carry, c=c):
            first(c, t).wait_recv()
            return carry

        lax.fori_loop(1, n, take_first, 0)

        def stage_one(g, carry, c=c):
            r0 = pl.multiple_of(g * 8, 8)
            for h in range(width // LANES):
                cols = pl.ds(h * LANES, LANES)
                planes = [
                    (recv[c, d, 0, pl.ds(r0, 8), cols], recv[c, d, 1, pl.ds(r0, 8), cols])
                    for d in range(n)
                ]
                for q, (ar, ai) in enumerate(butterflies(planes)):
                    if q == 0:
                        br, bi = ar, ai
                    else:
                        tr = tw_ref[0, pl.ds(q, 1), cols]
                        ti = tw_ref[1, pl.ds(q, 1), cols]
                        br = ar * tr - ai * ti
                        bi = ar * ti + ai * tr
                    right = pl.ds(width + h * LANES, LANES)
                    mid[q, pl.ds(r0, 8), cols] = br
                    mid[q, pl.ds(r0, 8), right] = -bi
                    mid[q, pl.ds(rows + r0, 8), cols] = bi
                    mid[q, pl.ds(rows + r0, 8), right] = br
            return carry

        lax.fori_loop(0, rows // 8, stage_one, 0)

        def stage_two(q, carry):
            value = mid[q]
            high = value.astype(jnp.bfloat16)
            low = (value - high.astype(jnp.float32)).astype(jnp.bfloat16)
            nt = (((1,), (1,)), ((), ()))
            dot = functools.partial(
                lax.dot_general, dimension_numbers=nt, preferred_element_type=jnp.float32
            )
            total = dot(whi_ref[...], high) + (dot(whi_ref[...], low) + dot(wlo_ref[...], high))
            spread[pl.ds(q, width, stride=n), pl.ds(0, 2 * rows)] = total
            return carry

        if n <= 16:
            for q in range(n):
                stage_two(q, 0)
        else:
            lax.fori_loop(0, n, stage_two, 0)

        def turn(owner):
            start = pl.multiple_of(owner * width, width)
            block = spread[pl.ds(start, width), :].T
            done[c, owner, 0] = block[:rows]
            done[c, owner, 1] = block[rows : 2 * rows]

        def send_second(t, carry, c=c):
            turn(lax.rem(me + t, n))
            second(c, t).start()
            return carry

        lax.fori_loop(1, n, send_second, 0)
        turn(me)
        own_out(c).start()

    for c in range(chunks):
        own_out(c).wait()

        def finish(t, carry, c=c):
            first(c, t).wait_send()
            second(c, t).wait_send()
            second(c, t).wait_recv()
            return carry

        lax.fori_loop(1, n, finish, 0)


def transform(slab, n):
    _, rows_total, width = slab.shape
    length = width * n
    rows_here = rows_total // n
    chunks = 2 if rows_here % 16 == 0 else 1
    rows = rows_here // chunks
    lanes = max(LANES, 2 * rows)
    k0 = np.arange(n)[:, None] * np.arange(width)[None, :]
    angle = 2.0 * np.pi * (k0 % length) / length
    twiddle = np.stack([np.cos(angle), -np.sin(angle)]).astype(np.float32)
    k1 = np.arange(width)[:, None] * np.arange(width)[None, :]
    angle = 2.0 * np.pi * (k1 % width) / width
    table = np.concatenate([np.cos(angle), -np.sin(angle)], axis=1) / math.sqrt(length)
    table_high = table.astype(np.float32).astype(ml_dtypes.bfloat16)
    table_low = (table - table_high.astype(np.float64)).astype(np.float32)
    table_low = table_low.astype(ml_dtypes.bfloat16)
    sem = pltpu.SemaphoreType.DMA
    return pl.pallas_call(
        functools.partial(kernel, n, chunks, rows),
        out_shape=jax.ShapeDtypeStruct(slab.shape, jnp.float32),
        in_specs=[pl.BlockSpec(memory_space=pl.ANY)]
        + [pl.BlockSpec(memory_space=pltpu.VMEM)] * 3,
        out_specs=pl.BlockSpec(memory_space=pl.ANY),
        scratch_shapes=[
            pltpu.VMEM((chunks, n, 2, rows, width), jnp.float32),
            pltpu.VMEM((n, 2 * rows, 2 * width), jnp.float32),
            pltpu.VMEM((length, lanes), jnp.float32),
            pltpu.VMEM((chunks, n, 2, rows, width), jnp.float32),
            sem((chunks, n)),
            sem((chunks, n)),
            sem((chunks, n)),
            sem((chunks, n)),
            sem((chunks,)),
            sem((chunks,)),
        ],
        compiler_params=pltpu.CompilerParams(
            collective_id=0, has_side_effects=True, vmem_limit_bytes=48 * 1024 * 1024
        ),
    )(slab, jnp.asarray(twiddle), jnp.asarray(table_high), jnp.asarray(table_low))


def shards(slab, block_on, block_band, band_gain):
    n = lax.axis_size("col")
    _, rows_total, width = slab.shape
    spectrum = transform(slab, n)
    choose = (block_band[..., None] == jnp.arange(band_gain.shape[0], dtype=jnp.int32)).astype(
        jnp.float32
    )
    weight = block_on.astype(jnp.float32) * jnp.sum(choose * band_gain, axis=-1)
    row_blocks = rows_total // BLOCK
    col_blocks = width // BLOCK
    masked = (
        spectrum.reshape(2, row_blocks, BLOCK, col_blocks, BLOCK) * weight[None, :, None, :, None]
    )
    return masked.reshape(2, rows_total, width)


def solution(mesh):
    placed = (P(None, "groups", "col"), P("groups", "col"), P("groups", "col"), P())
    return jax.shard_map(
        shards, mesh=mesh, in_specs=placed, out_specs=P(None, "groups", "col"), check_vma=False
    )
```

time: 139 us -> 100 us (0.72)
  Pallas kernels: 0 us -> 96.5 us
  waiting for transfers between devices: 94.1 us -> 0 us
  local copies, waits for them, and re-layouts: 16.8 us -> 0.51 us
  matrix products: 12.7 us -> 0 us
  starting transfers between devices: 11.6 us -> 0 us
    pallas_call x0 -> x1, Pallas kernels: none -> 96.5 us  [transform(): pl.pallas_call(functools.partial(kernel, n, chunks, rows), out_shape=jax....]
    all_to_all x2 -> x0, waiting for transfers between devices: 94.1 us -> none  [the longest x1 47.3 us: shards(): lax.all_to_all(slab.reshape(2, devices, rows_here, shard_cols), 'col', sp...]
    dot_general x8 -> x0, matrix products: 12.7 us -> none  [the longest x2 3.8 us: contract(): jnp.einsum(formula, stacked[0], cosine_table, precision=lax.Precision.HIG...]
    all_to_all x2 -> x0, starting transfers between devices: 11.6 us -> none  [the longest x1 6.55 us: shards(): lax.all_to_all(slab.reshape(2, devices, rows_here, shard_cols), 'col', sp...]
    another operation x4 -> x0, local copies, waits for them, and re-layouts: 4.98 us -> none  [contract(): return jnp.stack([real_part, imag_part])]
    squeeze x2 -> x0, local copies, waits for them, and re-layouts: 3.96 us -> none  [the longest x1 2.66 us: contract(): stacked[1]]
    slice x3 -> x0, local copies, waits for them, and re-layouts: 3.69 us -> none  [the longest x2 3.1 us: contract(): stacked[1]]
    reshape x1 -> x0, local copies, waits for them, and re-layouts: 3.13 us -> none  [shards(): slab.reshape(2, devices, rows_here, shard_cols)]
  transfers between devices with their start and end apart: 2 -> 0, of which waited for: 2 -> 0; matrix products, arithmetic and copies ran while one was open for 0% -> 0% of each run, Pallas kernels for 0% -> 0%
where the time goes in v1:
time: 100 us
  Pallas kernels  96.5 us (96%)
  other arithmetic  3.13 us (3%)
    pallas_call x1, Pallas kernels, transform(): pl.pallas_call(functools.partial(kernel, n, chunks, rows), out_shape=jax....  96.5 us

profile of v1, /device:TPU:13, one launch (start us, length us, event | category | flops | bytes accessed | tf_op | source)
XLA Modules:
  0.0 100.2 jit_solution(2942982299533726309)
XLA Ops:
  0.0 0.0 copy-start.1
  0.0 0.0 copy-start.2
  0.0 0.0 copy-start.3
  0.0 0.0 copy-start
  0.0 0.9 select_reduce_fusion
  0.9 0.7 convert_multiply_fusion
  1.6 0.1 copy.10
  1.7 0.3 mul.27
  2.1 0.1 copy.13
  2.1 0.0 copy-done.1
  2.1 0.0 copy-done.2
  2.2 0.0 copy-done.3
  2.2 0.0 copy-done
  2.2 96.5 %shard_map.73 = f32[2,1024,256]{2,1,0:T(8,128)S(1)} custom-call(f32[2,1024,256]{2,1,0:T(8,128)S(1)} %copy-done, f32[2,16,256]{2,1,0:T(8,128)S(1)} %copy-done.3, bf16[256,512]{1,0:T(8,128)(2,1)S(1)} %copy-done.2, bf16[256,512]{1,0:T(8,128)(2,1)S(1)} %copy-done.1), custom_call_target="tpu_custom_call" | custom-call | tf_op jit(solution)/shard_map/pallas_call | solution.py:203
  98.7 1.5 %broadcast_multiply_fusion = f32[2,1024,256]{2,1,0:T(8,128)} fusion(f32[2,1024,256]{2,1,0:T(8,128)S(1)} %shard_map.73, f32[1024,256]{1,0:T(8,128)S(1)} %bitcast.5), kind=kLoop, calls=%fused_computation.1 | loop fusion | flops 524288 | bytes 5242880 | tf_op jit(solution)/shard_map/mul | solution.py:238
Async XLA Ops:
  0.0 2.1 %copy-start.1 = (bf16[256,512]{1,0:T(8,128)(2,1)S(1)}, bf16[256,512]{1,0:T(8,128)(2,1)}, u32[]{:S(2)}) copy-start(bf16[256,512]{1,0:T(8,128)(2,1)} %constant.11.clone.wlo_ref) | copy-start | bytes 786436
  0.0 2.1 %copy-start.2 = (bf16[256,512]{1,0:T(8,128)(2,1)S(1)}, bf16[256,512]{1,0:T(8,128)(2,1)}, u32[]{:S(2)}) copy-start(bf16[256,512]{1,0:T(8,128)(2,1)} %constant.10.clone.whi_ref) | copy-start | bytes 786436
  0.0 2.2 %copy-start.3 = (f32[2,16,256]{2,1,0:T(8,128)S(1)}, f32[2,16,256]{2,1,0:T(8,128)}, u32[]{:S(2)}) copy-start(f32[2,16,256]{2,1,0:T(8,128)} %constant.9.clone.tw_ref) | copy-start | bytes 98308
  0.0 2.2 %copy-start = (f32[2,1024,256]{2,1,0:T(8,128)S(1)}, f32[2,1024,256]{2,1,0:T(8,128)}, u32[]{:S(2)}) copy-start(f32[2,1024,256]{2,1,0:T(8,128)} %x_ref.1) | copy-start | bytes 6291460

commit v2 on v1

--- a/solution.py
+++ b/solution.py
@@ -190,15 +190,6 @@
     chunks = 2 if rows_here % 16 == 0 else 1
     rows = rows_here // chunks
     lanes = max(LANES, 2 * rows)
-    k0 = np.arange(n)[:, None] * np.arange(width)[None, :]
-    angle = 2.0 * np.pi * (k0 % length) / length
-    twiddle = np.stack([np.cos(angle), -np.sin(angle)]).astype(np.float32)
-    k1 = np.arange(width)[:, None] * np.arange(width)[None, :]
-    angle = 2.0 * np.pi * (k1 % width) / width
-    table = np.concatenate([np.cos(angle), -np.sin(angle)], axis=1) / math.sqrt(length)
-    table_high = table.astype(np.float32).astype(ml_dtypes.bfloat16)
-    table_low = (table - table_high.astype(np.float64)).astype(np.float32)
-    table_low = table_low.astype(ml_dtypes.bfloat16)
     sem = pltpu.SemaphoreType.DMA
     return pl.pallas_call(
         functools.partial(kernel, n, chunks, rows),
@@ -221,12 +212,381 @@
         compiler_params=pltpu.CompilerParams(
             collective_id=0, has_side_effects=True, vmem_limit_bytes=48 * 1024 * 1024
         ),
-    )(slab, jnp.asarray(twiddle), jnp.asarray(table_high), jnp.asarray(table_low))
+    )(slab, *tables(n, width))
+
+
+def packed_kernel(
+    n, groups, chunks, blocks, sub, halves, keep,
+    x_ref, on_ref, tw_ref, whi_ref, wlo_ref, out_ref, rest_ref, flag_ref,
+    recv, mid, spread, units, send, infos, table,
+    s1, r1, s2, r2, si, ri, own1, own2, own3, own4,
+):
+    me = lax.axis_index("col")
+    flat = lax.axis_index("groups") * n + me
+    everyone = groups * n
+    width = halves * LANES
+    per = blocks // chunks
+    rows = per * sub
+    slots = blocks * halves
+
+    def place(i):
+        dev = lax.rem(flat + i, everyone)
+        return {"groups": dev // n, "col": lax.rem(dev, n)}
+
+    barrier = pltpu.get_barrier_semaphore()
+
+    def greet(i, carry):
+        pl.semaphore_signal(barrier, inc=1, device_id=place(i), device_id_type=MESH)
+        return carry
+
+    lax.fori_loop(1, everyone, greet, 0)
+
+    def part(owner, c):
+        return x_ref.at[:, pl.ds(c * per, per), owner]
+
+    def first(c, t):
+        peer = lax.rem(me + t, n)
+        return pltpu.make_async_remote_copy(
+            src_ref=part(peer, c),
+            dst_ref=recv.at[c, me],
+            send_sem=s1.at[c, t],
+            recv_sem=r1.at[c, t],
+            device_id={"col": peer},
+            device_id_type=MESH,
+        )
+
+    def second(t):
+        peer = lax.rem(me + t, n)
+        return pltpu.make_async_remote_copy(
+            src_ref=send.at[peer, pl.ds(0, keep)],
+            dst_ref=out_ref.at[me],
+            send_sem=s2.at[t],
+            recv_sem=r2.at[t],
+            device_id={"col": peer},
+            device_id_type=MESH,
+        )
+
+    def tell(i):
+        return pltpu.make_async_remote_copy(
+            src_ref=infos.at[flat],
+            dst_ref=infos.at[flat],
+            send_sem=si.at[i],
+            recv_sem=ri.at[i],
+            device_id=place(i),
+            device_id_type=MESH,
+        )
+
+    def own_in(c):
+        return pltpu.make_async_copy(part(me, c), recv.at[c, me], own1.at[c])
+
+    def own_out():
+        return pltpu.make_async_copy(send.at[me, pl.ds(0, keep)], out_ref.at[me], own2)
+
+    def own_rest(owner):
+        return pltpu.make_async_copy(
+            send.at[owner, pl.ds(keep, slots - keep)], rest_ref.at[owner], own3.at[owner]
+        )
+
+    for c in range(chunks):
+        own_in(c).start()
+    pl.semaphore_wait(barrier, everyone - 1)
+
+    def turned(i):
+        return 1 + lax.rem(i + n // 2, n - 1)
+
+    for c in range(chunks):
+
+        def send_first(i, carry, c=c):
+            first(c, turned(i)).start()
+            return carry
+
+        lax.fori_loop(0, n - 1, send_first, 0)
+
+    ons = [on_ref[u // halves, u % halves] for u in range(slots)]
+    ranks, count = [], jnp.int32(0)
+    for u in range(slots):
+        ranks.append(count)
+        count = count + ons[u]
+    lane = lax.broadcasted_iota(jnp.int32, (1, LANES), 1)
+    row = jnp.where(lane == slots, count, 0)
+    for u in range(slots):
+        hit = (lane == ranks[u]) & (lane < slots)
+        row = row + jnp.where(hit, u * ons[u], 0)
+    infos[flat] = row
+
+    def tell_all(i, carry):
+        tell(i).start()
+        return carry
+
+    lax.fori_loop(1, everyone, tell_all, 0)
+
+    def hear_all(i, carry):
+        tell(i).wait_recv()
+        return carry
+
+    lax.fori_loop(1, everyone, hear_all, 0)
+    fetch = pltpu.make_async_copy(infos, table, own4)
+    fetch.start()
+    fetch.wait()
+    most = jnp.int32(0)
+    for i in range(everyone):
+        most = jnp.maximum(most, table[i, 0, slots])
+    flag_ref[0, 0] = most
+
+    for c in range(chunks):
+        own_in(c).wait()
+
+        def take_first(t, carry, c=c):
+            first(c, t).wait_recv()
+            return carry
+
+        lax.fori_loop(1, n, take_first, 0)
+
+        def stage_one(a, carry, c=c):
+            r0 = pl.multiple_of(c * 2 * rows + a * sub, sub)
+            for h in range(halves):
+                cols = pl.ds(h * LANES, LANES)
+                planes = [(recv[c, d, 0, a, :, cols], recv[c, d, 1, a, :, cols]) for d in range(n)]
+                for q, (ar, ai) in enumerate(butterflies(planes)):
+                    if q == 0:
+                        br, bi = ar, ai
+                    else:
+                        tr = tw_ref[0, pl.ds(q, 1), cols]
+                        ti = tw_ref[1, pl.ds(q, 1), cols]
+                        br = ar * tr - ai * ti
+                        bi = ar * ti + ai * tr
+                    right = pl.ds(width + h * LANES, LANES)
+                    mid[q, pl.ds(r0, sub), cols] = br
+                    mid[q, pl.ds(r0, sub), right] = -bi
+                    mid[q, pl.ds(rows + r0, sub), cols] = bi
+                    mid[q, pl.ds(rows + r0, sub), right] = br
+            return carry
+
+        lax.fori_loop(0, per, stage_one, 0)
+
+    for q in range(n):
+        value = mid[q]
+        high = value.astype(jnp.bfloat16)
+        low = (value - high.astype(jnp.float32)).astype(jnp.bfloat16)
+        dot = functools.partial(
+            lax.dot_general,
+            dimension_numbers=(((1,), (1,)), ((), ())),
+            preferred_element_type=jnp.float32,
+        )
+        total = dot(whi_ref[...], high) + (dot(whi_ref[...], low) + dot(wlo_ref[...], high))
+        spread[pl.ds(q, width, stride=n), :] = total
+
+    def turn(owner):
+        start = pl.multiple_of(owner * width, width)
+        block = spread[pl.ds(start, width), :].T
+        for c in range(chunks):
+            for part_index in range(2):
+                for a in range(per):
+                    r0 = (c * 2 + part_index) * rows + a * sub
+                    for h in range(halves):
+                        units[(c * per + a) * halves + h, part_index] = block[
+                            r0 : r0 + sub, h * LANES : (h + 1) * LANES
+                        ]
+        base = (flat - me) + owner
+        for i in range(slots):
+            send[owner, i] = units[table[base, 0, i]]
+
+    def send_second(i, carry):
+        t = turned(i)
+        peer = lax.rem(me + t, n)
+        turn(peer)
+        second(t).start()
+        own_rest(peer).start()
+        return carry
+
+    lax.fori_loop(0, n - 1, send_second, 0)
+    turn(me)
+    own_out().start()
+    own_rest(me).start()
+    own_out().wait()
+
+    def drain(i, carry):
+        own_rest(i).wait()
+        return carry
+
+    lax.fori_loop(0, n, drain, 0)
+
+    def quiet(i, carry):
+        tell(i).wait_send()
+        return carry
+
+    lax.fori_loop(1, everyone, quiet, 0)
+
+    def finish(t, carry):
+        for c in range(chunks):
+            first(c, t).wait_send()
+        second(t).wait_send()
+        second(t).wait_recv()
+        return carry
+
+    lax.fori_loop(1, n, finish, 0)
+
+
+def rest_kernel(n, rest_ref, out_ref, s1, r1, own):
+    me = lax.axis_index("col")
+    barrier = pltpu.get_barrier_semaphore()
+
+    def greet(t, carry):
+        pl.semaphore_signal(
+            barrier, inc=1, device_id={"col": lax.rem(me + t, n)}, device_id_type=MESH
+        )
+        return carry
+
+    lax.fori_loop(1, n, greet, 0)
+    mine = pltpu.make_async_copy(rest_ref.at[me], out_ref.at[me], own)
+    mine.start()
+    pl.semaphore_wait(barrier, n - 1)
+
+    def copy(t):
+        peer = lax.rem(me + t, n)
+        return pltpu.make_async_remote_copy(
+            src_ref=rest_ref.at[peer],
+            dst_ref=out_ref.at[me],
+            send_sem=s1.at[t],
+            recv_sem=r1.at[t],
+            device_id={"col": peer},
+            device_id_type=MESH,
+        )
+
+    def begin(t, carry):
+        copy(t).start()
+        return carry
+
+    def end(t, carry):
+        copy(t).wait()
+        return carry
+
+    lax.fori_loop(1, n, begin, 0)
+    lax.fori_loop(1, n, end, 0)
+    mine.wait()
+
+
+def unpack_kernel(n, blocks, sub, halves, keep, on_ref, band_ref, gain_ref, got_ref, more_ref, out_ref):
+    rank = jnp.int32(0)
+    a = pl.program_id(0)
+    slots = blocks * halves
+    for u in range(slots):
+        rank = rank + jnp.where(u < a * halves, on_ref[u // halves, u % halves], 0)
+    for h in range(halves):
+        on = on_ref[a, h]
+        gain = gain_ref[band_ref[a, h]]
+        cols = pl.ds(h * LANES, LANES)
+
+        def take(ref, slot):
+            for d in range(n):
+                for part_index in range(2):
+                    value = ref[d, slot, part_index]
+                    out_ref[part_index, 0, d, :, cols] = value * gain
+
+        @pl.when((on != 0) & (rank < keep))
+        def _():
+            take(got_ref, rank)
+
+        @pl.when((on != 0) & (rank >= keep))
+        def _():
+            take(more_ref, rank - keep)
+
+        @pl.when(on == 0)
+        def _():
+            out_ref[:, 0, :, :, cols] = jnp.zeros((2, n, sub, LANES), jnp.float32)
+
+        rank = rank + on
+
+
+def tables(n, width):
+    length = n * width
+    k0 = np.arange(n)[:, None] * np.arange(width)[None, :]
+    angle = 2.0 * np.pi * (k0 % length) / length
+    twiddle = np.stack([np.cos(angle), -np.sin(angle)]).astype(np.float32)
+    k1 = np.arange(width)[:, None] * np.arange(width)[None, :]
+    angle = 2.0 * np.pi * (k1 % width) / width
+    table = np.concatenate([np.cos(angle), -np.sin(angle)], axis=1) / math.sqrt(length)
+    high = table.astype(np.float32).astype(ml_dtypes.bfloat16)
+    low = (table - high.astype(np.float64)).astype(np.float32).astype(ml_dtypes.bfloat16)
+    return jnp.asarray(twiddle), jnp.asarray(high), jnp.asarray(low)
+
+
+def packed(slab, block_on, block_band, band_gain):
+    n, groups = lax.axis_size("col"), lax.axis_size("groups")
+    _, rows_total, width = slab.shape
+    blocks, halves = rows_total // BLOCK, width // LANES
+    sub = BLOCK // n
+    chunks = 2
+    per = blocks // chunks
+    slots = blocks * halves
+    keep = 3 * slots // 4
+    sem = pltpu.SemaphoreType.DMA
+    anywhere = pl.BlockSpec(memory_space=pl.ANY)
+    vmem = pl.BlockSpec(memory_space=pltpu.VMEM)
+    smem = pl.BlockSpec(memory_space=pltpu.SMEM)
+    f32 = jnp.float32
+    unit = (2, sub, LANES)
+    everyone = n * groups
+    got, rest, flag = pl.pallas_call(
+        functools.partial(packed_kernel, n, groups, chunks, blocks, sub, halves, keep),
+        out_shape=(
+            jax.ShapeDtypeStruct((n, keep) + unit, f32),
+            jax.ShapeDtypeStruct((n, slots - keep) + unit, f32),
+            jax.ShapeDtypeStruct((1, 1), jnp.int32),
+        ),
+        in_specs=[anywhere, smem, vmem, vmem, vmem],
+        out_specs=(anywhere, anywhere, smem),
+        scratch_shapes=[
+            pltpu.VMEM((chunks, n, 2, per, sub, width), f32),
+            pltpu.VMEM((n, 2 * blocks * sub, 2 * width), f32),
+            pltpu.VMEM((n * width, 2 * blocks * sub), f32),
+            pltpu.VMEM((slots,) + unit, f32),
+            pltpu.VMEM((n, slots) + unit, f32),
+            pltpu.VMEM((everyone, 1, LANES), jnp.int32),
+            pltpu.SMEM((everyone, 1, LANES), jnp.int32),
+            sem((chunks, n)),
+            sem((chunks, n)),
+            sem((n,)),
+            sem((n,)),
+            sem((everyone,)),
+            sem((everyone,)),
+            sem((chunks,)),
+            sem,
+            sem((n,)),
+            sem,
+        ],
+        compiler_params=pltpu.CompilerParams(
+            collective_id=1, has_side_effects=True, vmem_limit_bytes=40 * 1024 * 1024
+        ),
+    )(slab.reshape(2, blocks, n, sub, width), block_on, *tables(n, width))
+
+    def fetch_rest(rest):
+        return pl.pallas_call(
+            functools.partial(rest_kernel, n),
+            out_shape=jax.ShapeDtypeStruct(rest.shape, f32),
+            in_specs=[anywhere],
+            out_specs=anywhere,
+            scratch_shapes=[sem((n,)), sem((n,)), sem],
+            compiler_params=pltpu.CompilerParams(collective_id=2, has_side_effects=True),
+        )(rest)
+
+    more = lax.cond(flag[0, 0] > keep, fetch_rest, lambda rest: rest, rest)
+    out = pl.pallas_call(
+        functools.partial(unpack_kernel, n, blocks, sub, halves, keep),
+        out_shape=jax.ShapeDtypeStruct((2, blocks, n, sub, width), f32),
+        grid=(blocks,),
+        in_specs=[smem, smem, smem, vmem, vmem],
+        out_specs=pl.BlockSpec((2, 1, n, sub, width), lambda a: (0, a, 0, 0, 0)),
+        compiler_params=pltpu.CompilerParams(vmem_limit_bytes=16 * 1024 * 1024),
+    )(block_on, block_band, band_gain, got, more)
+    return out.reshape(slab.shape)
 
 
 def shards(slab, block_on, block_band, band_gain):
     n = lax.axis_size("col")
     _, rows_total, width = slab.shape
+    if BLOCK % (8 * n) == 0 and rows_total % (2 * BLOCK) == 0:
+        return packed(slab, block_on, block_band, band_gain)
     spectrum = transform(slab, n)
     choose = (block_band[..., None] == jnp.arange(band_gain.shape[0], dtype=jnp.int32)).astype(
         jnp.float32

time: 100 us -> 109 us (1.090)
  the two profiles are of different devices: /device:TPU:13 before, /device:TPU:0 now
where the time goes in v2:
time: 109 us
  Pallas kernels  102 us (94%)
  local copies, waits for them, and re-layouts  5.76 us (5%)
    pallas_call x1, Pallas kernels, packed(): pl.pallas_call(functools.partial(packed_kernel, n, groups, chunks, blocks...  98.5 us
    unnamed x12, local copies, waits for them, and re-layouts  5.76 us
    pallas_call x1, Pallas kernels, packed(): pl.pallas_call(functools.partial(unpack_kernel, n, blocks, sub, halves, k...  3.91 us

profile of v2, /device:TPU:0, one launch (start us, length us, event | category | flops | bytes accessed | tf_op | source)
XLA Modules:
  0.0 108.9 jit_solution(8277566307787116255)
XLA Ops:
  0.0 0.8 copy.9.on_ref
  0.8 0.8 copy.10.band_ref
  1.5 0.0 copy-start
  1.5 1.6 %copy-done = f32[2,1024,256]{2,1,0:T(8,128)S(1)} copy-done((f32[2,1024,256]{2,1,0:T(8,128)S(1)}, f32[2,1024,256]{2,1,0:T(8,128)}, u32[]{:S(2)}) %copy-start) | copy-done | bytes 2097176
  3.1 0.0 copy-start.1
  3.1 0.9 copy-done.1
  4.0 0.0 copy-start.2
  4.1 0.9 copy-done.2
  5.0 0.0 copy-start.3
  5.0 0.8 copy-done.3
  5.8 0.0 copy-start.4
  5.8 98.5 %shard_map.73 = (f32[16,12,2,8,128]{4,3,2,1,0:T(8,128)S(1)}, f32[16,4,2,8,128]{4,3,2,1,0:T(8,128)S(1)}, s32[1,1]{1,0:T(1,128)}) custom-call(f32[2,8,16,8,256]{4,3,2,1,0:T(8,128)S(1)} %bitcast.3, s32[8,2]{1,0:T(8,128)S(1)} %copy.9.on_ref, f32[2,16,256]{2,1,0:T(8,128)S(1)} %copy-done.3, bf16[256,512]{1,0:T(8,128)(2,1)S(1)} %copy-done.2, ...), custom_call_target="tpu_custom_call" | custom-call | tf_op jit(solution)/shard_map/pallas_call | solution.py:530
  105.0 0.0 copy-done.4
  105.0 3.9 %shard_map.74 = f32[2,8,16,8,256]{4,3,2,1,0:T(8,128)} custom-call(s32[8,2]{1,0:T(8,128)S(1)} %copy.9.on_ref, s32[8,2]{1,0:T(8,128)S(1)} %copy.10.band_ref, f32[4]{0:T(128)S(1)} %copy-done.4, f32[16,12,2,8,128]{4,3,2,1,0:T(8,128)S(1)} %get-tuple-element.13.got_ref, f32[16,4,2,8,128]{4,3,2,1,0:T(8,128)S(1)} %get-tuple-element.16.more_ref), custom_call_target="tpu_custom_call" | custom-call | tf_op jit(solution)/shard_map/pallas_call | solution.py:574
  (1 shorter events, 0.0 us)
Async XLA Ops:
  1.5 1.6 %copy-start = (f32[2,1024,256]{2,1,0:T(8,128)S(1)}, f32[2,1024,256]{2,1,0:T(8,128)}, u32[]{:S(2)}) copy-start(f32[2,1024,256]{2,1,0:T(8,128)} %param.9) | copy-start | bytes 6291460
  3.1 0.9 copy-start.1
  4.0 0.9 copy-start.2
  5.0 0.8 copy-start.3
  5.8 99.2 %copy-start.4 = (f32[4]{0:T(128)S(1)}, f32[4]{0:T(128)}, u32[]{:S(2)}) copy-start(f32[4]{0:T(128)} %gain_ref.1) | copy-start | bytes 52

commit v3 on v1

--- a/solution.py
+++ b/solution.py
@@ -209,7 +209,7 @@
         scratch_shapes=[
             pltpu.VMEM((chunks, n, 2, rows, width), jnp.float32),
             pltpu.VMEM((n, 2 * rows, 2 * width), jnp.float32),
-            pltpu.VMEM((length, lanes), jnp.float32),
+            pltpu.VMEM((length + n, lanes), jnp.float32),
             pltpu.VMEM((chunks, n, 2, rows, width), jnp.float32),
             sem((chunks, n)),
             sem((chunks, n)),

time: 100 us -> 100 us (level)
  no operation moved by 1% of the time
where the time goes in v3:
time: 100 us
  Pallas kernels  96.5 us (96%)
  other arithmetic  3.13 us (3%)
    pallas_call x1, Pallas kernels, transform(): pl.pallas_call(functools.partial(kernel, n, chunks, rows), out_shape=jax....  96.5 us

profile of v3, /device:TPU:13, one launch (start us, length us, event | category | flops | bytes accessed | tf_op | source)
XLA Modules:
  0.0 100.2 jit_solution(15691370923711153244)
XLA Ops:
  0.0 0.0 copy-start.1
  0.0 0.0 copy-start.2
  0.0 0.0 copy-start.3
  0.0 0.0 copy-start
  0.0 0.9 select_reduce_fusion
  0.9 0.7 convert_multiply_fusion
  1.6 0.1 copy.10
  1.7 0.3 mul.27
  2.1 0.1 copy.13
  2.1 0.0 copy-done.1
  2.1 0.0 copy-done.2
  2.2 0.0 copy-done.3
  2.2 0.0 copy-done
  2.2 96.5 %shard_map.73 = f32[2,1024,256]{2,1,0:T(8,128)S(1)} custom-call(f32[2,1024,256]{2,1,0:T(8,128)S(1)} %copy-done, f32[2,16,256]{2,1,0:T(8,128)S(1)} %copy-done.3, bf16[256,512]{1,0:T(8,128)(2,1)S(1)} %copy-done.2, bf16[256,512]{1,0:T(8,128)(2,1)S(1)} %copy-done.1), custom_call_target="tpu_custom_call" | custom-call | tf_op jit(solution)/shard_map/pallas_call | solution.py:203
  98.7 1.5 %broadcast_multiply_fusion = f32[2,1024,256]{2,1,0:T(8,128)} fusion(f32[2,1024,256]{2,1,0:T(8,128)S(1)} %shard_map.73, f32[1024,256]{1,0:T(8,128)S(1)} %bitcast.5), kind=kLoop, calls=%fused_computation.1 | loop fusion | flops 524288 | bytes 5242880 | tf_op jit(solution)/shard_map/mul | solution.py:238
Async XLA Ops:
  0.0 2.1 %copy-start.1 = (bf16[256,512]{1,0:T(8,128)(2,1)S(1)}, bf16[256,512]{1,0:T(8,128)(2,1)}, u32[]{:S(2)}) copy-start(bf16[256,512]{1,0:T(8,128)(2,1)} %constant.11.clone.wlo_ref) | copy-start | bytes 786436
  0.0 2.1 %copy-start.2 = (bf16[256,512]{1,0:T(8,128)(2,1)S(1)}, bf16[256,512]{1,0:T(8,128)(2,1)}, u32[]{:S(2)}) copy-start(bf16[256,512]{1,0:T(8,128)(2,1)} %constant.10.clone.whi_ref) | copy-start | bytes 786436
  0.0 2.2 %copy-start.3 = (f32[2,16,256]{2,1,0:T(8,128)S(1)}, f32[2,16,256]{2,1,0:T(8,128)}, u32[]{:S(2)}) copy-start(f32[2,16,256]{2,1,0:T(8,128)} %constant.9.clone.tw_ref) | copy-start | bytes 98308
  0.0 2.2 %copy-start = (f32[2,1024,256]{2,1,0:T(8,128)S(1)}, f32[2,1024,256]{2,1,0:T(8,128)}, u32[]{:S(2)}) copy-start(f32[2,1024,256]{2,1,0:T(8,128)} %x_ref.1) | copy-start | bytes 6291460
